TPU v7x, 32 devices: a whole 2x2x4 slice. The times are simulated.
32 devices in a mesh: rep: 2 (over x), yz: 8 (over z, y), gx: 2 (over core).
Axes of the slice: x: 2, y: 2, z: 4, core: 2. Of those that a mesh axis runs over, the one named last changes fastest.
Arguments:
- tokens: bfloat16 [64, 3, 18432], P(('rep', 'yz'), None, 'gx'), parts along dimension 0, may hold values from -6 to 6
- query_weight: bfloat16 [18432, 2048], P('gx', 'yz'), may hold values from -0.046875 to 0.046875
- key_weight: bfloat16 [18432, 256], P('gx', 'yz'), may hold values from -0.3125 to 0.3125
- value_weight: bfloat16 [18432, 256], P('gx', 'yz'), may hold values from -0.046875 to 0.046875
- out_weight: bfloat16 [2048, 18432], P('yz', 'gx'), may hold values from -0.125 to 0.125
- key_cache: bfloat16 [64, 1536, 256], P(('rep', 'yz', 'gx')), parts along dimension 0, may hold values from -600 to 600
- value_cache: bfloat16 [64, 1536, 256], P(('rep', 'yz', 'gx')), parts along dimension 0, may hold values from -6 to 6
- lengths: int32 [64], P(('rep', 'yz', 'gx')), parts along dimension 0, may hold values from 192 to 1536, as said below
Outputs:
- attended: bfloat16 [64, 3, 18432], P(('rep', 'yz'), None, 'gx'), parts along dimension 0
There are 2 independent parts, one for each index of `rep`. A program takes and returns all parts, laid end to end along the dimension named above; an argument that names none is the same for every part. Nothing has to cross between parts.
Inputs may be any that keep to these rules, and one draw needn't show every extreme that they name: `lengths`: each row has at least 192 live cached positions; some row has all 1536.
All inputs are finite; a program needn't handle non-finite values.
Results may differ from a plain program's by a relative error of at most 0.014.
The roundings to bfloat16 on the way count: a program that leaves them out, or rounds other values in their place, can miss the bound.
Values may be sent and summed in bfloat16 or wider, within the bound.
A program may use at most 128 MiB of HBM per device.

v0:
```python
import math

import jax
import jax.numpy as jnp
from jax import lax
from jax.sharding import PartitionSpec as P

HD = 256
STEPS = 3


def rotate(values, positions):
    half_dim = values.shape[-1] // 2
    frequency = jnp.exp(jnp.arange(half_dim, dtype=jnp.float32) * (-math.log(10000.0) / half_dim))
    angles = positions[..., None] * frequency
    cosine = jnp.cos(angles)
    sine_part = jnp.sin(angles)
    front_half = values[..., :half_dim]
    back_half = values[..., half_dim:]
    return jnp.concatenate(
        [front_half * cosine - back_half * sine_part, back_half * cosine + front_half * sine_part],
        axis=-1,
    )


def normalize(cache_scores, new_scores, lengths, steps_count):
    cache_len = cache_scores.shape[-1]
    cache_live = (jnp.arange(cache_len, dtype=jnp.int32)[None, :] < lengths[:, None])[
        :, None, None, :
    ]
    new_live = (
        jnp.arange(steps_count, dtype=jnp.int32)[None, :]
        <= jnp.arange(steps_count, dtype=jnp.int32)[:, None]
    )[None, :, None, :]
    floor_value = jnp.float32(-1e30)
    cache_scores = jnp.where(cache_live, cache_scores, floor_value)
    new_scores = jnp.where(new_live, new_scores, floor_value)
    highest = jnp.maximum(
        jnp.max(cache_scores, axis=-1, keepdims=True), jnp.max(new_scores, axis=-1, keepdims=True)
    )
    cache_exp = jnp.exp(cache_scores - highest)
    new_exp = jnp.exp(new_scores - highest)
    denominator = jnp.sum(cache_exp, axis=-1, keepdims=True) + jnp.sum(
        new_exp, axis=-1, keepdims=True
    )
    return (
        (cache_exp / denominator).astype(jnp.bfloat16),
        (new_exp / denominator).astype(jnp.bfloat16),
    )


def local(
    tokens, query_weight, key_weight, value_weight, out_weight, key_cache, value_cache, lengths
):
    yz_count = lax.axis_size("yz")
    gx_count = lax.axis_size("gx")
    rows_here = lengths.shape[0]
    gathered = lax.all_gather(tokens, "yz", axis=0, tiled=True)
    all_rows = gathered.shape[0]
    flattened = gathered.reshape(all_rows * STEPS, gathered.shape[2])
    query_part = jnp.dot(flattened, query_weight, preferred_element_type=jnp.float32)
    key_part = jnp.dot(flattened, key_weight, preferred_element_type=jnp.float32)
    value_part = jnp.dot(flattened, value_weight, preferred_element_type=jnp.float32)
    arrived = (
        lax.all_to_all(
            query_part.reshape(yz_count * gx_count, rows_here, STEPS, 1, query_part.shape[1]),
            ("yz", "gx"),
            split_axis=0,
            concat_axis=3,
            tiled=True,
        ),
        lax.all_to_all(
            key_part.reshape(yz_count * gx_count, rows_here, STEPS, 1, key_part.shape[1]),
            ("yz", "gx"),
            split_axis=0,
            concat_axis=3,
            tiled=True,
        ),
        lax.all_to_all(
            value_part.reshape(yz_count * gx_count, rows_here, STEPS, 1, value_part.shape[1]),
            ("yz", "gx"),
            split_axis=0,
            concat_axis=3,
            tiled=True,
        ),
    )
    totals = [
        jnp.sum(member.reshape(rows_here, STEPS, yz_count, gx_count, member.shape[-1]), axis=3)
        for member in arrived
    ]
    queries = totals[0]
    key_sum = totals[1].reshape(rows_here, STEPS, HD)
    new_values = totals[2].reshape(rows_here, STEPS, HD).astype(jnp.bfloat16)
    positions = (lengths[:, None] + jnp.arange(STEPS, dtype=jnp.int32)[None, :]).astype(jnp.float32)
    rot_queries = rotate(queries, positions[:, :, None]).astype(jnp.bfloat16)
    new_keys = rotate(key_sum, positions).astype(jnp.bfloat16)
    scale_factor = HD ** (-0.5)
    cache_scores = (
        jnp.einsum("rshd,rkd->rshk", rot_queries, key_cache, preferred_element_type=jnp.float32)
        * scale_factor
    )
    new_scores = (
        jnp.einsum("rshd,rtd->rsht", rot_queries, new_keys, preferred_element_type=jnp.float32)
        * scale_factor
    )
    cache_probs, new_probs = normalize(cache_scores, new_scores, lengths, STEPS)
    head_out = jnp.einsum(
        "rshk,rkd->rshd", cache_probs, value_cache, preferred_element_type=jnp.float32
    )
    head_out = head_out + jnp.einsum(
        "rsht,rtd->rshd", new_probs, new_values, preferred_element_type=jnp.float32
    )
    head_out = head_out.astype(jnp.bfloat16)
    returned = lax.all_to_all(head_out, "yz", split_axis=2, concat_axis=0, tiled=True)
    paired = lax.all_gather(
        returned.reshape(yz_count, 1, rows_here, STEPS, HD), "gx", axis=1, tiled=True
    )
    head_rows = paired.reshape(all_rows, STEPS, HD)
    row_count = tokens.shape[0] * lax.axis_size("yz")
    product = jnp.dot(
        head_rows.reshape(row_count * STEPS, HD), out_weight, preferred_element_type=jnp.float32
    )
    return lax.psum_scatter(
        product.reshape(row_count, STEPS, out_weight.shape[1]).astype(jnp.bfloat16),
        "yz",
        scatter_dimension=0,
        tiled=True,
    )


def solution(mesh):
    placed = (
        P(("rep", "yz"), None, "gx"),
        P("gx", "yz"),
        P("gx", "yz"),
        P("gx", "yz"),
        P("yz", "gx"),
        P(("rep", "yz", "gx"), None, None),
        P(("rep", "yz", "gx"), None, None),
        P(("rep", "yz", "gx")),
    )
    return jax.shard_map(
        local, mesh=mesh, in_specs=placed, out_specs=P(("rep", "yz"), None, "gx"), check_vma=False
    )
```

profile of v0, /device:TPU:0, one launch (start us, length us, event | category | flops | bytes accessed | tf_op | source)
XLA Modules:
  0.0 218.8 jit_solution(13006653506755319426)
XLA Ops:
  6.5 0.0 copy-start
  6.5 0.0 all-gather.3.cloned.1.call-start
  6.5 1.9 copy.34
  8.5 0.0 all-gather.3.cloned.1.call-update
  8.5 0.0 copy-start.2
  8.5 0.8 add_convert_fusion.2
  9.3 0.7 iota_compare_fusion
  10.0 54.3 %all-gather.3.cloned.1.call-done = bf16[32,3,9216]{2,1,0:T(4,128)(2,1)} async-done(((bf16[4,3,9216]{2,1,0:T(4,128)(2,1)}), bf16[32,3,9216]{2,1,0:T(4,128)(2,1)}) %all-gather.3.cloned.1.call-update) | async-done | bytes 1769488 | tf_op jit(solution)/shard_map/all_gather | solution.py:58
  64.4 3.2 %convolution_bitcast_fusion.1 = f32[16,2,3,1,32]{4,0,2,1,3:T(8,128)S(1)} fusion(bf16[16,2,3,9216]{3,2,1,0:T(4,128)(2,1)} %bitcast.87, bf16[9216,32]{0,1:T(8,128)(2,1)} %param.10), kind=kOutput, calls=%fused_computation.12 | convolution fusion | flops 56623104 | bytes 2371584 | tf_op jit(solution)/shard_map/dot_general | solution.py:62
  67.6 0.7 reshape.168
  68.3 3.5 %all-to-all-start.1 = ((f32[16,1,192]{2,1,0:T(1,128)}), f32[16,1,192]{2,1,0:T(1,128)S(1)}, u32[]{:S(2)}, u32[]{:S(2)}) async-start(f32[16,1,192]{2,1,0:T(1,128)} %reshape.168), calls=%async_computation.1 | async-start | bytes 32768 | tf_op jit(solution)/shard_map/all_to_all | solution.py:72
  71.8 0.0 copy-done.2
  71.8 3.1 %convolution_bitcast_fusion = f32[16,2,3,1,32]{4,0,2,1,3:T(8,128)S(1)} fusion(bf16[16,2,3,9216]{3,2,1,0:T(4,128)(2,1)} %bitcast.88, bf16[9216,32]{0,1:T(8,128)(2,1)S(1)} %copy-done.2), kind=kOutput, calls=%fused_computation.11 | convolution fusion | flops 56623104 | bytes 2371584 | tf_op jit(solution)/shard_map/dot_general | solution.py:63
  74.9 0.7 reshape.170
  75.6 2.6 %all-to-all-done.1 = f32[16,1,192]{2,1,0:T(1,128)S(1)} async-done(((f32[16,1,192]{2,1,0:T(1,128)}), f32[16,1,192]{2,1,0:T(1,128)S(1)}, u32[]{:S(2)}, u32[]{:S(2)}) %all-to-all-start.1) | async-done | bytes 12320 | tf_op jit(solution)/shard_map/all_to_all | solution.py:72
  78.3 3.4 %all-to-all-start.2 = ((f32[16,1,192]{2,1,0:T(1,128)}), f32[16,1,192]{2,1,0:T(1,128)S(1)}, u32[]{:S(2)}, u32[]{:S(2)}) async-start(f32[16,1,192]{2,1,0:T(1,128)} %reshape.170), calls=%async_computation.2 | async-start | bytes 32768 | tf_op jit(solution)/shard_map/all_to_all | solution.py:79
  81.7 4.7 %fusion.7 = f32[16,2,3,1,256]{4,0,2,1,3:T(8,128)S(1)} fusion(bf16[9216,256]{1,0:T(8,128)(2,1)} %param.9, bf16[16,2,3,9216]{3,2,1,0:T(4,128)(2,1)} %bitcast.89), kind=kOutput, calls=%fused_computation.9 | convolution fusion | flops 452984832 | bytes 6586368 | tf_op jit(solution)/shard_map/dot_general | solution.py:61
  86.3 0.7 copy.37
  87.1 0.0 copy-start.1
  87.1 0.6 broadcast.73
  87.7 0.7 reduce
  88.4 0.1 reshape.169
  88.5 0.1 reshape.162
  88.6 0.0 all-to-all-done.2
  88.6 6.0 %all-to-all-start = ((f32[16,2,3,1,256]{4,1,3,2,0:T(2,128)}), f32[16,2,3,1,256]{4,1,3,2,0:T(2,128)S(1)}, u32[]{:S(2)}, u32[]{:S(2)}) async-start(f32[16,2,3,1,256]{4,1,3,2,0:T(2,128)} %copy.37), calls=%async_computation | async-start | bytes 196608 | tf_op jit(solution)/shard_map/all_to_all | solution.py:65
  94.6 0.0 all-reduce.3.cloned.1.call-start
  94.7 0.7 reduce.1
  95.4 0.1 reshape.171
  95.6 0.1 reshape.160
  95.7 0.1 subtract_convert_fusion.1
  95.8 6.3 %all-to-all-done = f32[16,2,3,1,256]{4,1,3,2,0:T(2,128)S(1)} async-done(((f32[16,2,3,1,256]{4,1,3,2,0:T(2,128)}), f32[16,2,3,1,256]{4,1,3,2,0:T(2,128)S(1)}, u32[]{:S(2)}, u32[]{:S(2)}) %all-to-all-start) | async-done | bytes 98336 | tf_op jit(solution)/shard_map/all_to_all | solution.py:65
  102.0 0.1 reduce_sum.45
  102.1 0.0 copy-done
  102.1 0.6 fusion.35
  102.8 0.2 fusion.36
  103.0 0.2 fusion.22
  103.2 0.2 fusion.26
  103.4 0.0 copy-done.1
  103.4 0.4 fusion.13
  103.8 9.0 %all_to_all.60 = bf16[2,3,8,256]{3,0,1,2:T(2,128)(2,1)S(1)} all-to-all(bf16[2,3,8,256]{3,0,1,2:T(2,128)(2,1)S(1)} %copy.52), channel_id=1, replica_groups=mesh['rep'=2,'yz'=8,'gx'=2] {'yz'}, dimensions={2} | all-to-all | bytes 49152 | tf_op jit(solution)/shard_map/all_to_all | solution.py:114
  112.8 1.8 all-gather
  114.7 4.4 %convolution_convert_fusion = bf16[32,3,9216]{2,0,1:T(8,128)(2,1)} fusion(bf16[32,3,256]{2,0,1:T(8,128)(2,1)S(1)} %dot_general.45, bf16[256,9216]{1,0:T(8,128)(2,1)} %param.12), kind=kOutput, calls=%fused_computation | convolution fusion | flops 453869568 | bytes 6537216 | tf_op jit(solution)/shard_map/dot_general | solution.py:120
  119.1 0.0 copy-start.3
  119.1 0.0 all-reduce.3.cloned.1.call-update
  119.1 0.6 copy-done.3
  119.8 0.6 dynamic-slice
  121.0 89.2 %all-reduce.3.cloned.1.call-done = bf16[32,3,9216]{2,0,1:T(8,128)(2,1)} async-done(((bf16[32,3,9216]{2,0,1:T(8,128)(2,1)}), bf16[32,3,9216]{2,0,1:T(8,128)(2,1)}) %all-reduce.3.cloned.1.call-update) | async-done | bytes 1769488
  210.1 1.8 constant_dynamic-slice_fusion
  (17 shorter events, 0.3 us)
Async XLA Ops:
  6.5 95.6 %copy-start = (bf16[2,1536,256]{2,1,0:T(8,128)(2,1)S(1)}, bf16[2,1536,256]{2,1,0:T(8,128)(2,1)}, u32[]{:S(2)}) copy-start(bf16[2,1536,256]{2,1,0:T(8,128)(2,1)} %param.13) | copy-start | bytes 4718596
  6.5 57.8 %all-gather.3.cloned.1.call-start = ((), (), s32[]{:S(2)}) async-start(), calls=%async_computation.4 | async-start | bytes 2654208 | tf_op jit(solution)/shard_map/all_gather | solution.py:58
  8.5 63.3 %copy-start.2 = (bf16[9216,32]{0,1:T(8,128)(2,1)S(1)}, bf16[9216,32]{0,1:T(8,128)(2,1)}, u32[]{:S(2)}) copy-start(bf16[9216,32]{0,1:T(8,128)(2,1)} %param.11) | copy-start | bytes 1769476
  68.3 10.0 %all-to-all-start.1 = ((f32[16,1,192]{2,1,0:T(1,128)}), f32[16,1,192]{2,1,0:T(1,128)S(1)}, u32[]{:S(2)}, u32[]{:S(2)}) async-start(f32[16,1,192]{2,1,0:T(1,128)} %reshape.168), calls=%async_computation.1 | async-start | bytes 32768 | tf_op jit(solution)/shard_map/all_to_all | solution.py:72
  78.3 10.4 %all-to-all-start.2 = ((f32[16,1,192]{2,1,0:T(1,128)}), f32[16,1,192]{2,1,0:T(1,128)S(1)}, u32[]{:S(2)}, u32[]{:S(2)}) async-start(f32[16,1,192]{2,1,0:T(1,128)} %reshape.170), calls=%async_computation.2 | async-start | bytes 32768 | tf_op jit(solution)/shard_map/all_to_all | solution.py:79
  87.1 16.3 %copy-start.1 = (bf16[2,1536,256]{2,1,0:T(8,128)(2,1)S(1)}, bf16[2,1536,256]{2,1,0:T(8,128)(2,1)}, u32[]{:S(2)}) copy-start(bf16[2,1536,256]{2,1,0:T(8,128)(2,1)} %param.14) | copy-start | bytes 4718596
  88.6 13.4 %all-to-all-start = ((f32[16,2,3,1,256]{4,1,3,2,0:T(2,128)}), f32[16,2,3,1,256]{4,1,3,2,0:T(2,128)S(1)}, u32[]{:S(2)}, u32[]{:S(2)}) async-start(f32[16,2,3,1,256]{4,1,3,2,0:T(2,128)} %copy.37), calls=%async_computation | async-start | bytes 196608 | tf_op jit(solution)/shard_map/all_to_all | solution.py:65
  94.6 115.5 %all-reduce.3.cloned.1.call-start = ((), (), s32[]{:S(2)}) async-start(), calls=%async_computation.5 | async-start | bytes 3538944
  119.1 0.7 copy-start.3
Sparse Core Ops, SparseCore 0:
  9.5 54.7 all-gather.2
  119.2 90.8 all-reduce.2
where the time goes:
time: 219 us
  waiting for transfers between devices  152 us (69%)
  matrix products  16.7 us (8%)
  between operations  14.3 us (7%)
  starting transfers between devices  12.9 us (6%)
  blocking collectives  10.8 us (5%)
  local copies, waits for them, and re-layouts  8.2 us (4%)
  other arithmetic  3.49 us (2%)
    unnamed x3, waiting for transfers between devices  89.2 us
    all_gather x1, waiting for transfers between devices, local(): gathered = lax.all_gather(tokens, 'yz', axis=0, tiled=True)  54.3 us
    all_to_all x1, blocking collectives, local(): lax.all_to_all(head_out, 'yz', split_axis=2, concat_axis=0, tiled=True)  9 us
    unnamed x17, local copies, waits for them, and re-layouts  6.58 us
    all_to_all x1, waiting for transfers between devices, local(): lax.all_to_all(query_part.reshape(yz_count * gx_count, rows_here, STEPS,...  6.25 us
    all_to_all x1, starting transfers between devices, local(): lax.all_to_all(query_part.reshape(yz_count * gx_count, rows_here, STEPS,...  5.98 us
    dot_general x1, matrix products, local(): jnp.dot(flattened, query_weight, preferred_element_type=jnp.float32)  4.66 us
    dot_general x1, matrix products, local(): jnp.dot(head_rows.reshape(row_count * STEPS, HD), out_weight, preferred_e...  4.42 us
  transfers between devices with their start and end apart: 5, of which 4 were waited for; matrix products, arithmetic and copies ran while one was open for 6% of the time, Pallas kernels for 0%

commit v1 on v0

--- a/solution.py
+++ b/solution.py
@@ -3,6 +3,8 @@
 import jax
 import jax.numpy as jnp
 from jax import lax
+from jax.experimental import pallas as pl
+from jax.experimental.pallas import tpu as pltpu
 from jax.sharding import PartitionSpec as P
 
 HD = 256
@@ -128,7 +130,416 @@
     )
 
 
+FOLD = 4
+CHUNKS = 3
+NZ = 4
+NY = 2
+MESH = pl.DeviceIdType.MESH
+
+
+def place():
+    me = lax.axis_index("yz")
+    return me // NY, me % NY
+
+
+def greet(z, y):
+    barrier = pltpu.get_barrier_semaphore()
+    pl.semaphore_signal(barrier, inc=1, device_id={"yz": z * NY + 1 - y}, device_id_type=MESH)
+
+    @pl.when(z > 0)
+    def _():
+        pl.semaphore_signal(barrier, inc=1, device_id={"yz": (z - 1) * NY + y}, device_id_type=MESH)
+
+    @pl.when(z < NZ - 1)
+    def _():
+        pl.semaphore_signal(barrier, inc=1, device_id={"yz": (z + 1) * NY + y}, device_id_type=MESH)
+
+    pl.semaphore_wait(barrier, jnp.where(jnp.logical_and(z > 0, z < NZ - 1), 3, 2))
+
+
+def gather_project_kernel(
+    tokens_ref, qw_ref, kw_ref, vw_ref, q_out, k_out, v_out,
+    gathered, qw, kw, vw, w_sem, own_sem, up_send, down_send, side_send, recv,
+):
+    z, y = place()
+    width = gathered.shape[3]
+    rows = gathered.shape[2]
+    features = qw.shape[0] // FOLD
+    loads = [
+        pltpu.make_async_copy(source, target, w_sem.at[i])
+        for i, (source, target) in enumerate(((qw_ref, qw), (kw_ref, kw), (vw_ref, vw)))
+    ]
+    own = [
+        pltpu.make_async_copy(
+            tokens_ref.at[:, pl.ds(c * width, width)], gathered.at[c, z * NY + y], own_sem.at[c]
+        )
+        for c in range(CHUNKS)
+    ]
+    for copy in own:
+        copy.start()
+    greet(z, y)
+
+    def block(c, origin_z, origin_y, target, sem):
+        origin = origin_z * NY + origin_y
+        return pltpu.make_async_remote_copy(
+            src_ref=gathered.at[c, origin],
+            dst_ref=gathered.at[c, origin],
+            send_sem=sem.at[c, origin_z],
+            recv_sem=recv.at[c, origin],
+            device_id={"yz": target},
+            device_id_type=MESH,
+        )
+
+    side = z * NY + 1 - y
+
+    def up(c, origin_z):
+        return block(c, origin_z, y, (z + 1) * NY + y, up_send)
+
+    def down(c, origin_z):
+        return block(c, origin_z, y, (z - 1) * NY + y, down_send)
+
+    def across(c, origin_z):
+        return block(c, origin_z, y, side, side_send)
+
+    def arrival(c, origin_z, origin_y):
+        block(c, origin_z, origin_y, side, side_send).wait_recv()
+
+    for c in range(CHUNKS):
+        own[c].wait()
+
+        @pl.when(z < NZ - 1)
+        def _(c=c):
+            up(c, z).start()
+
+        @pl.when(z > 0)
+        def _(c=c):
+            down(c, z).start()
+
+        across(c, z).start()
+    for copy in loads:
+        copy.start()
+
+    def forward(c):
+        for k in range(1, NZ):
+            @pl.when(z >= k)
+            def _(k=k):
+                arrival(c, z - k, y)
+
+                @pl.when(z < NZ - 1)
+                def _():
+                    up(c, z - k).start()
+
+                across(c, z - k).start()
+
+            @pl.when(z + k < NZ)
+            def _(k=k):
+                arrival(c, z + k, y)
+
+                @pl.when(z > 0)
+                def _():
+                    down(c, z + k).start()
+
+                across(c, z + k).start()
+
+    def multiply(c):
+        for origin_z in range(NZ):
+            arrival(c, origin_z, 1 - y)
+        block_rows = gathered[c].reshape(NZ * NY * rows, width)
+        fold = (lax.broadcasted_iota(jnp.int32, (NZ * NY * rows, 1), 0) % rows) // (rows // FOLD)
+        for out, weight in ((q_out, qw), (k_out, kw), (v_out, vw)):
+            total = None
+            for f in range(FOLD):
+                term = jnp.dot(
+                    block_rows,
+                    weight[pl.ds(f * features + c * width, width), :],
+                    preferred_element_type=jnp.float32,
+                )
+                total = term if f == 0 else jnp.where(fold == f, term, total)
+            if c == 0:
+                out[...] = total
+            else:
+                out[...] += total
+
+    for c in range(CHUNKS):
+        forward(c)
+        if c == 1:
+            for copy in loads:
+                copy.wait()
+        if c > 0:
+            multiply(c - 1)
+    multiply(CHUNKS - 1)
+
+    for c in range(CHUNKS):
+        for origin_z in range(NZ):
+            across(c, origin_z).wait_send()
+
+            @pl.when(jnp.logical_and(z < NZ - 1, origin_z <= z))
+            def _(c=c, origin_z=origin_z):
+                up(c, origin_z).wait_send()
+
+            @pl.when(jnp.logical_and(z > 0, origin_z >= z))
+            def _(c=c, origin_z=origin_z):
+                down(c, origin_z).wait_send()
+
+
+def gather_project(folded, query_weight, key_weight, value_weight):
+    rows, features = folded.shape
+    width = features // CHUNKS
+    count = NZ * NY
+    outs = [w.shape[1] for w in (query_weight, key_weight, value_weight)]
+    hbm = pl.BlockSpec(memory_space=pl.ANY)
+    vmem = pl.BlockSpec(memory_space=pltpu.VMEM)
+    dma = pltpu.SemaphoreType.DMA
+    return pl.pallas_call(
+        gather_project_kernel,
+        out_shape=[jax.ShapeDtypeStruct((count * rows, n), jnp.float32) for n in outs],
+        in_specs=[hbm] * 4,
+        out_specs=[vmem] * 3,
+        scratch_shapes=[
+            pltpu.VMEM((CHUNKS, count, rows, width), jnp.bfloat16),
+            pltpu.VMEM(query_weight.shape, jnp.bfloat16),
+            pltpu.VMEM(key_weight.shape, jnp.bfloat16),
+            pltpu.VMEM(value_weight.shape, jnp.bfloat16),
+            dma((3,)),
+            dma((CHUNKS,)),
+            dma((CHUNKS, NZ)),
+            dma((CHUNKS, NZ)),
+            dma((CHUNKS, NZ)),
+            dma((CHUNKS, count)),
+        ],
+        compiler_params=pltpu.CompilerParams(
+            collective_id=0, has_side_effects=True, vmem_limit_bytes=48 * 1024 * 1024
+        ),
+        name="gather_project",
+    )(folded, query_weight, key_weight, value_weight)
+
+
+def project_scatter_kernel(
+    heads_ref, weight_ref, out_ref,
+    weight, terms, side_in, up_in, down_in,
+    w_sem, side_send, side_recv, line_send, up_recv, down_recv,
+):
+    z, y = place()
+    rows, width = terms.shape[2], terms.shape[3]
+    depth = weight_ref.shape[0]
+    features = weight_ref.shape[1] // FOLD
+    loads = [
+        [
+            pltpu.make_async_copy(
+                weight_ref.at[:, pl.ds(f * features + c * width, width)],
+                weight.at[c, pl.ds(f * depth, depth), :],
+                w_sem.at[c, f],
+            )
+            for f in range(FOLD)
+        ]
+        for c in range(CHUNKS)
+    ]
+    for group in loads:
+        for copy in group:
+            copy.start()
+    greet(z, y)
+
+    def across(c, dest):
+        return pltpu.make_async_remote_copy(
+            src_ref=terms.at[c, dest * NY + 1 - y],
+            dst_ref=side_in.at[c, dest],
+            send_sem=side_send.at[c, dest],
+            recv_sem=side_recv.at[c, dest],
+            device_id={"yz": z * NY + 1 - y},
+            device_id_type=MESH,
+        )
+
+    def along(c, dest, step):
+        return pltpu.make_async_remote_copy(
+            src_ref=terms.at[c, dest * NY + y],
+            dst_ref=(up_in if step > 0 else down_in).at[c, dest],
+            send_sem=line_send.at[c, dest],
+            recv_sem=(up_recv if step > 0 else down_recv).at[c, dest],
+            device_id={"yz": (z + step) * NY + y},
+            device_id_type=MESH,
+        )
+
+    for c in range(CHUNKS):
+        for copy in loads[c]:
+            copy.wait()
+        product = jnp.dot(heads_ref[...], weight[c], preferred_element_type=jnp.float32)
+        terms[c] = product.astype(jnp.bfloat16).reshape(NZ * NY, rows, width)
+        for k in range(NZ - 1, 0, -1):
+            @pl.when(z + k < NZ)
+            def _(c=c, k=k):
+                across(c, z + k).start()
+
+            @pl.when(z >= k)
+            def _(c=c, k=k):
+                across(c, z - k).start()
+
+        across(c, z).start()
+
+    def own_pair(c, dest):
+        across(c, dest).wait_recv()
+        return terms[c, dest * NY + y].astype(jnp.float32) + side_in[c, dest].astype(jnp.float32)
+
+    def pass_on(c, dest, step, has_source):
+        arrived = up_in if step > 0 else down_in
+        total = own_pair(c, dest)
+        terms[c, dest * NY + y] = total.astype(jnp.bfloat16)
+
+        @pl.when(has_source)
+        def _():
+            along(c, dest, step).wait_recv()
+            terms[c, dest * NY + y] = (total + arrived[c, dest].astype(jnp.float32)).astype(
+                jnp.bfloat16
+            )
+
+        along(c, dest, step).start()
+
+    for c in range(CHUNKS):
+        for k in range(NZ - 1, 0, -1):
+            @pl.when(z + k < NZ)
+            def _(c=c, k=k):
+                pass_on(c, z + k, 1, z > 0)
+
+            @pl.when(z >= k)
+            def _(c=c, k=k):
+                pass_on(c, z - k, -1, z < NZ - 1)
+
+        here = pl.ds(c * width, width)
+        total = own_pair(c, z)
+
+        @pl.when(z == 0)
+        def _(c=c, here=here, total=total):
+            along(c, z, -1).wait_recv()
+            out_ref[:, here] = (total + down_in[c, z].astype(jnp.float32)).astype(jnp.bfloat16)
+
+        @pl.when(z == NZ - 1)
+        def _(c=c, here=here, total=total):
+            along(c, z, 1).wait_recv()
+            out_ref[:, here] = (total + up_in[c, z].astype(jnp.float32)).astype(jnp.bfloat16)
+
+        @pl.when(jnp.logical_and(z > 0, z < NZ - 1))
+        def _(c=c, here=here, total=total):
+            along(c, z, 1).wait_recv()
+            along(c, z, -1).wait_recv()
+            out_ref[:, here] = (
+                total + up_in[c, z].astype(jnp.float32) + down_in[c, z].astype(jnp.float32)
+            ).astype(jnp.bfloat16)
+
+    for c in range(CHUNKS):
+        for dest in range(NZ):
+            across(c, dest).wait_send()
+
+            @pl.when(dest != z)
+            def _(c=c, dest=dest):
+                along(c, dest, 1).wait_send()
+
+
+def project_scatter(heads, out_weight):
+    depth, columns = out_weight.shape
+    count = NZ * NY
+    rows = heads.shape[0] // count
+    width = columns // FOLD // CHUNKS
+    dma = pltpu.SemaphoreType.DMA
+    vmem = pl.BlockSpec(memory_space=pltpu.VMEM)
+    landing = pltpu.VMEM((CHUNKS, NZ, rows, width), jnp.bfloat16)
+    sems = dma((CHUNKS, NZ))
+    return pl.pallas_call(
+        project_scatter_kernel,
+        out_shape=jax.ShapeDtypeStruct((rows, columns // FOLD), jnp.bfloat16),
+        in_specs=[vmem, pl.BlockSpec(memory_space=pl.ANY)],
+        out_specs=vmem,
+        scratch_shapes=[
+            pltpu.VMEM((CHUNKS, FOLD * depth, width), jnp.bfloat16),
+            pltpu.VMEM((CHUNKS, count, rows, width), jnp.bfloat16),
+            landing,
+            landing,
+            landing,
+            dma((CHUNKS, FOLD)),
+            sems,
+            sems,
+            sems,
+            sems,
+            sems,
+        ],
+        compiler_params=pltpu.CompilerParams(
+            collective_id=1, has_side_effects=True, vmem_limit_bytes=48 * 1024 * 1024
+        ),
+        name="project_scatter",
+    )(heads, out_weight)
+
+
+def attend(queries, key_sum, new_values, key_cache, value_cache, lengths):
+    positions = (lengths[:, None] + jnp.arange(STEPS, dtype=jnp.int32)[None, :]).astype(jnp.float32)
+    rot_queries = rotate(queries, positions[:, :, None]).astype(jnp.bfloat16)
+    new_keys = rotate(key_sum, positions).astype(jnp.bfloat16)
+    scale_factor = HD ** (-0.5)
+    cache_scores = (
+        jnp.einsum("rshd,rkd->rshk", rot_queries, key_cache, preferred_element_type=jnp.float32)
+        * scale_factor
+    )
+    new_scores = (
+        jnp.einsum("rshd,rtd->rsht", rot_queries, new_keys, preferred_element_type=jnp.float32)
+        * scale_factor
+    )
+    cache_probs, new_probs = normalize(cache_scores, new_scores, lengths, STEPS)
+    head_out = jnp.einsum(
+        "rshk,rkd->rshd", cache_probs, value_cache, preferred_element_type=jnp.float32
+    )
+    head_out = head_out + jnp.einsum(
+        "rsht,rtd->rshd", new_probs, new_values, preferred_element_type=jnp.float32
+    )
+    return head_out.astype(jnp.bfloat16)
+
+
+def local_line(
+    tokens, query_weight, key_weight, value_weight, out_weight, key_cache, value_cache, lengths
+):
+    yz_count = lax.axis_size("yz")
+    gx_count = lax.axis_size("gx")
+    rows_here = lengths.shape[0]
+    owned = tokens.shape[0] * STEPS
+    features = tokens.shape[2]
+    folded = (
+        tokens.reshape(owned, FOLD, features // FOLD)
+        .transpose(1, 0, 2)
+        .reshape(FOLD * owned, features // FOLD)
+    )
+    parts = gather_project(folded, query_weight, key_weight, value_weight)
+    joined = jnp.concatenate(parts, axis=1)
+    joined = joined.reshape(yz_count, FOLD, owned, joined.shape[1]).sum(axis=1)
+    arrived = lax.all_to_all(
+        joined.reshape(yz_count * gx_count, rows_here * STEPS, joined.shape[-1]),
+        ("yz", "gx"),
+        split_axis=0,
+        concat_axis=0,
+        tiled=True,
+    )
+    totals = arrived.reshape(yz_count, gx_count, rows_here, STEPS, -1).sum(axis=1)
+    totals = totals.transpose(1, 2, 0, 3)
+    key_columns = key_weight.shape[1]
+    queries = totals[..., :HD]
+    key_sum = totals[..., HD : HD + key_columns].reshape(rows_here, STEPS, HD)
+    new_values = totals[..., HD + key_columns :].reshape(rows_here, STEPS, HD).astype(jnp.bfloat16)
+    head_out = attend(queries, key_sum, new_values, key_cache, value_cache, lengths)
+    by_head = head_out.reshape(rows_here * STEPS, yz_count, HD).transpose(1, 0, 2)
+    sent = jnp.broadcast_to(by_head[:, None], (yz_count, gx_count) + by_head.shape[1:])
+    returned = lax.all_to_all(
+        sent.reshape(yz_count * gx_count, rows_here * STEPS, HD),
+        ("yz", "gx"),
+        split_axis=0,
+        concat_axis=0,
+        tiled=True,
+    )
+    heads = returned.reshape(yz_count, 1, owned, 1, HD)
+    same = jnp.eye(FOLD, dtype=bool)[None, :, None, :, None]
+    heads = jnp.where(same, heads, jnp.bfloat16(0)).reshape(yz_count * FOLD * owned, FOLD * HD)
+    summed = project_scatter(heads, out_weight)
+    return (
+        summed.reshape(FOLD, owned, -1).transpose(1, 0, 2).reshape(tokens.shape[0], STEPS, features)
+    )
+
+
 def solution(mesh):
+    body = local_line if mesh.shape["yz"] == NZ * NY and mesh.shape["gx"] == 2 else local
     placed = (
         P(("rep", "yz"), None, "gx"),
         P("gx", "yz"),
@@ -140,5 +551,5 @@
         P(("rep", "yz", "gx")),
     )
     return jax.shard_map(
-        local, mesh=mesh, in_specs=placed, out_specs=P(("rep", "yz"), None, "gx"), check_vma=False
-    )
+        body, mesh=mesh, in_specs=placed, out_specs=P(("rep", "yz"), None, "gx"), check_vma=False
+    )

time: 219 us -> 108 us (0.49)
  waiting for transfers between devices: 152 us -> 15.7 us
  Pallas kernels: 0 us -> 67.4 us
  matrix products: 16.7 us -> 1.36 us
  between operations: 14.3 us -> 0.23 us
  blocking collectives: 10.8 us -> 0 us
  local copies, waits for them, and re-layouts: 8.2 us -> 13.8 us
  starting transfers between devices: 12.9 us -> 7.62 us
  other arithmetic: 3.49 us -> 1.1 us
    unnamed x3 -> x0, waiting for transfers between devices: 89.2 us -> none
    pallas_call x0 -> x2, Pallas kernels: none -> 67.4 us  [the longest x1 36.5 us: project_scatter(): pl.pallas_call(project_scatter_kernel, out_shape=jax.ShapeDtypeStruct((ro...]
    all_gather x1 -> x0, waiting for transfers between devices: 54.3 us -> none  [local(): gathered = lax.all_gather(tokens, 'yz', axis=0, tiled=True)]
    dot_general x8 -> x4, matrix products: 16.7 us -> 1.36 us  [the longest x1 0.61 us: attend(): jnp.einsum('rshd,rkd->rshk', rot_queries, key_cache, preferred_element_ty...]
    all_to_all x1 -> x0, blocking collectives: 9 us -> none  [local(): lax.all_to_all(head_out, 'yz', split_axis=2, concat_axis=0, tiled=True)]
    all_to_all x3 -> x2, waiting for transfers between devices: 8.86 us -> 15.7 us  [the longest x1 8.81 us: local_line(): lax.all_to_all(joined.reshape(yz_count * gx_count, rows_here * STEPS, joi...]
    all_to_all x3 -> x2, starting transfers between devices: 12.9 us -> 7.62 us  [the longest x1 4.12 us: local_line(): lax.all_to_all(joined.reshape(yz_count * gx_count, rows_here * STEPS, joi...]
    unnamed x17 -> x21, local copies, waits for them, and re-layouts: 6.58 us -> 10.8 us
  transfers between devices with their start and end apart: 5 -> 2, of which waited for: 4 -> 2; matrix products, arithmetic and copies ran while one was open for 6% -> 0% of each run, Pallas kernels for 0% -> 0%
where the time goes in v1:
time: 108 us; the launch traced here: 107 us
  Pallas kernels  67.4 us (62%)
  waiting for transfers between devices  15.7 us (15%)
  local copies, waits for them, and re-layouts  13.8 us (13%)
  starting transfers between devices  7.62 us (7%)
  matrix products  1.36 us (1%)
  other arithmetic  1.1 us (1%)
    pallas_call x1, Pallas kernels, project_scatter(): pl.pallas_call(project_scatter_kernel, out_shape=jax.ShapeDtypeStruct((ro...  36.5 us
    pallas_call x1, Pallas kernels, gather_project(): pl.pallas_call(gather_project_kernel, out_shape=[jax.ShapeDtypeStruct((co...  30.9 us
    unnamed x21, local copies, waits for them, and re-layouts  10.8 us
    all_to_all x1, waiting for transfers between devices, local_line(): lax.all_to_all(joined.reshape(yz_count * gx_count, rows_here * STEPS, joi...  8.81 us
    all_to_all x1, waiting for transfers between devices, local_line(): lax.all_to_all(sent.reshape(yz_count * gx_count, rows_here * STEPS, HD),...  6.85 us
    all_to_all x1, starting transfers between devices, local_line(): lax.all_to_all(joined.reshape(yz_count * gx_count, rows_here * STEPS, joi...  4.12 us
    all_to_all x1, starting transfers between devices, local_line(): lax.all_to_all(sent.reshape(yz_count * gx_count, rows_here * STEPS, HD),...  3.5 us
  transfers between devices with their start and end apart: 2, of which 2 were waited for; matrix products, arithmetic and copies ran while one was open for 0% of the time, Pallas kernels for 0%

profile of v1, /device:TPU:0, one launch (start us, length us, event | category | flops | bytes accessed | tf_op | source)
XLA Modules:
  0.0 107.2 jit_solution(12326727775024806899)
XLA Ops:
  0.0 0.0 copy-start
  0.0 0.0 copy-start.4
  0.0 2.9 %copy.14.kw_ref = bf16[9216,32]{1,0:T(8,128)(2,1)} copy(bf16[9216,32]{0,1:T(8,128)(2,1)} %param.10) | data formatting | bytes 1179648 | tf_op args[2]
  2.9 0.0 copy-done.4
  2.9 0.0 copy-start.5
  2.9 1.8 %copy.15.vw_ref = bf16[9216,32]{1,0:T(8,128)(2,1)} copy(bf16[9216,32]{0,1:T(8,128)(2,1)S(1)} %copy-done.4) | data formatting | bytes 1179648 | tf_op args[3]
  4.8 0.0 copy-done.5
  4.8 0.2 copy.12
  4.9 0.2 reshape.148
  5.2 0.1 reshape.149.tokens_ref
  5.2 0.0 copy-start.1
  5.2 1.7 %copy-done.1 = bf16[9216,32]{1,0:T(8,128)(2,1)S(1)} copy-done((bf16[9216,32]{1,0:T(8,128)(2,1)S(1)}, bf16[9216,32]{1,0:T(8,128)(2,1)}, u32[]{:S(2)}) %copy-start.1) | copy-done | bytes 589848
  6.9 0.0 copy-start.2
  6.9 1.7 %copy-done.2 = bf16[9216,32]{1,0:T(8,128)(2,1)S(1)} copy-done((bf16[9216,32]{1,0:T(8,128)(2,1)S(1)}, bf16[9216,32]{1,0:T(8,128)(2,1)}, u32[]{:S(2)}) %copy-start.2) | copy-done | bytes 589848
  8.6 30.9 %gather_project.1 = (f32[384,256]{1,0:T(8,128)S(1)}, f32[384,32]{1,0:T(8,128)S(1)}, f32[384,32]{1,0:T(8,128)S(1)}) custom-call(bf16[48,2304]{1,0:T(8,128)(2,1)S(1)} %reshape.149.tokens_ref, bf16[9216,256]{1,0:T(8,128)(2,1)} %qw_ref.1, bf16[9216,32]{1,0:T(8,128)(2,1)S(1)} %copy-done.1, bf16[9216,32]{1,0:T(8,128)(2,1)S(1)} %copy-done.2), custom_call_target="tpu_custom_call" | custom-call | tf_op jit(solution)/shard_map/gather_project/pallas_call | solution.py:293
  39.5 0.1 pad_maximum_fusion
  39.6 0.0 copy-start.6
  39.6 0.1 reshape.150
  39.7 0.1 reduce_sum.36
  39.8 0.7 reshape.151
  40.5 4.1 %all-to-all-start = ((f32[16,6,320]{2,1,0:T(8,128)}), f32[16,6,320]{2,1,0:T(8,128)S(1)}, u32[]{:S(2)}, u32[]{:S(2)}) async-start(f32[16,6,320]{2,1,0:T(8,128)} %reshape.151), calls=%async_computation | async-start | bytes 393216 | tf_op jit(solution)/shard_map/all_to_all | solution.py:509
  44.6 0.0 copy-done.6
  44.6 0.1 iota_compare_fusion
  44.7 0.1 add_convert_fusion.2
  44.8 0.0 copy-start.7
  44.8 8.8 %all-to-all-done = f32[16,6,320]{2,1,0:T(8,128)S(1)} async-done(((f32[16,6,320]{2,1,0:T(8,128)}), f32[16,6,320]{2,1,0:T(8,128)S(1)}, u32[]{:S(2)}, u32[]{:S(2)}) %all-to-all-start) | async-done | bytes 122912 | tf_op jit(solution)/shard_map/all_to_all | solution.py:509
  53.7 0.1 slice.43
  53.7 0.1 reshape.162
  53.8 0.1 subtract_convert_fusion.1
  54.0 0.0 copy-done
  54.0 0.6 fusion.23
  54.6 0.2 fusion.24
  54.8 0.2 fusion.11
  55.0 0.1 reshape.161
  55.1 0.2 fusion.15
  55.3 0.0 copy-done.7
  55.3 0.4 fusion.7
  55.7 0.6 broadcast_in_dim.73
  56.3 3.5 %all-to-all-start.1 = ((bf16[16,6,256]{2,1,0:T(8,128)(2,1)}), bf16[16,6,256]{2,1,0:T(8,128)(2,1)S(1)}, u32[]{:S(2)}, u32[]{:S(2)}) async-start(bf16[16,6,256]{2,1,0:T(8,128)(2,1)} %bitcast.14), calls=%async_computation.1 | async-start | bytes 131072 | tf_op jit(solution)/shard_map/all_to_all | solution.py:525
  59.9 6.8 %all-to-all-done.1 = bf16[16,6,256]{2,1,0:T(8,128)(2,1)S(1)} async-done(((bf16[16,6,256]{2,1,0:T(8,128)(2,1)}), bf16[16,6,256]{2,1,0:T(8,128)(2,1)S(1)}, u32[]{:S(2)}, u32[]{:S(2)}) %all-to-all-start.1) | async-done | bytes 49184 | tf_op jit(solution)/shard_map/all_to_all | solution.py:525
  66.7 0.4 broadcast_select_fusion
  67.1 0.2 copy.32
  67.2 0.0 copy-start.3
  67.3 2.3 %copy-done.3 = bf16[256,9216]{1,0:T(8,128)(2,1)S(1)} copy-done((bf16[256,9216]{1,0:T(8,128)(2,1)S(1)}, bf16[256,9216]{1,0:T(8,128)(2,1)}, u32[]{:S(2)}) %copy-start.3) | copy-done | bytes 4718616
  69.6 36.5 %project_scatter.1 = bf16[48,2304]{1,0:T(8,128)(2,1)S(1)} custom-call(bf16[384,1024]{1,0:T(8,128)(2,1)S(1)} %bitcast.44, bf16[256,9216]{1,0:T(8,128)(2,1)S(1)} %copy-done.3), custom_call_target="tpu_custom_call" | custom-call | tf_op jit(solution)/shard_map/project_scatter/pallas_call | solution.py:445
  106.1 0.1 reshape.156
  106.1 0.1 copy.23
  106.2 0.1 reshape.157
  106.3 0.8 copy.24
  (13 shorter events, 0.2 us)
Async XLA Ops:
  0.0 54.0 %copy-start = (bf16[2,1536,256]{2,1,0:T(8,128)(2,1)S(1)}, bf16[2,1536,256]{2,1,0:T(8,128)(2,1)}, u32[]{:S(2)}) copy-start(bf16[2,1536,256]{2,1,0:T(8,128)(2,1)} %param.13) | copy-start | bytes 4718596
  0.0 2.9 %copy-start.4 = (bf16[9216,32]{0,1:T(8,128)(2,1)S(1)}, bf16[9216,32]{0,1:T(8,128)(2,1)}, u32[]{:S(2)}) copy-start(bf16[9216,32]{0,1:T(8,128)(2,1)} %param.11) | copy-start | bytes 1769476
  2.9 1.8 %copy-start.5 = (bf16[4,3,9216]{2,0,1:T(4,128)(2,1)S(1)}, bf16[4,3,9216]{2,0,1:T(4,128)(2,1)}, u32[]{:S(2)}) copy-start(bf16[4,3,9216]{2,0,1:T(4,128)(2,1)} %param.8) | copy-start | bytes 663556
  5.2 1.7 %copy-start.1 = (bf16[9216,32]{1,0:T(8,128)(2,1)S(1)}, bf16[9216,32]{1,0:T(8,128)(2,1)}, u32[]{:S(2)}) copy-start(bf16[9216,32]{1,0:T(8,128)(2,1)} %copy.14.kw_ref) | copy-start | bytes 1769476
  6.9 1.7 %copy-start.2 = (bf16[9216,32]{1,0:T(8,128)(2,1)S(1)}, bf16[9216,32]{1,0:T(8,128)(2,1)}, u32[]{:S(2)}) copy-start(bf16[9216,32]{1,0:T(8,128)(2,1)} %copy.15.vw_ref) | copy-start | bytes 1769476
  39.6 5.0 %copy-start.6 = (s32[2]{0:T(128)S(1)}, s32[2]{0:T(128)}, u32[]{:S(2)}) copy-start(s32[2]{0:T(128)} %param.15) | copy-start | bytes 28
  40.5 13.1 %all-to-all-start = ((f32[16,6,320]{2,1,0:T(8,128)}), f32[16,6,320]{2,1,0:T(8,128)S(1)}, u32[]{:S(2)}, u32[]{:S(2)}) async-start(f32[16,6,320]{2,1,0:T(8,128)} %reshape.151), calls=%async_computation | async-start | bytes 393216 | tf_op jit(solution)/shard_map/all_to_all | solution.py:509
  44.8 10.5 %copy-start.7 = (bf16[2,1536,256]{2,1,0:T(8,128)(2,1)S(1)}, bf16[2,1536,256]{2,1,0:T(8,128)(2,1)}, u32[]{:S(2)}) copy-start(bf16[2,1536,256]{2,1,0:T(8,128)(2,1)} %param.14) | copy-start | bytes 4718596
  56.3 10.4 %all-to-all-start.1 = ((bf16[16,6,256]{2,1,0:T(8,128)(2,1)}), bf16[16,6,256]{2,1,0:T(8,128)(2,1)S(1)}, u32[]{:S(2)}, u32[]{:S(2)}) async-start(bf16[16,6,256]{2,1,0:T(8,128)(2,1)} %bitcast.14), calls=%async_computation.1 | async-start | bytes 131072 | tf_op jit(solution)/shard_map/all_to_all | solution.py:525
  67.2 2.3 %copy-start.3 = (bf16[256,9216]{1,0:T(8,128)(2,1)S(1)}, bf16[256,9216]{1,0:T(8,128)(2,1)}, u32[]{:S(2)}) copy-start(bf16[256,9216]{1,0:T(8,128)(2,1)} %weight_ref.1) | copy-start | bytes 14155780

commit v2 on v1

--- a/solution.py
+++ b/solution.py
@@ -132,6 +132,7 @@
 
 FOLD = 4
 CHUNKS = 3
+AHEAD = 3
 NZ = 4
 NY = 2
 MESH = pl.DeviceIdType.MESH
@@ -158,8 +159,8 @@
 
 
 def gather_project_kernel(
-    tokens_ref, qw_ref, kw_ref, vw_ref, q_out, k_out, v_out,
-    gathered, qw, kw, vw, w_sem, own_sem, up_send, down_send, side_send, recv,
+    tokens_ref, qw_ref, kw_ref, vw_ref, q_out, kv_out,
+    gathered, qw, kvw, w_sem, own_sem, up_send, down_send, side_send, recv,
 ):
     z, y = place()
     width = gathered.shape[3]
@@ -167,7 +168,13 @@
     features = qw.shape[0] // FOLD
     loads = [
         pltpu.make_async_copy(source, target, w_sem.at[i])
-        for i, (source, target) in enumerate(((qw_ref, qw), (kw_ref, kw), (vw_ref, vw)))
+        for i, (source, target) in enumerate(
+            (
+                (qw_ref, qw),
+                (kw_ref, kvw.at[pl.ds(0, kw_ref.shape[0]), :]),
+                (vw_ref, kvw.at[pl.ds(kw_ref.shape[0], vw_ref.shape[0]), :]),
+            )
+        )
     ]
     own = [
         pltpu.make_async_copy(
@@ -246,19 +253,26 @@
             arrival(c, origin_z, 1 - y)
         block_rows = gathered[c].reshape(NZ * NY * rows, width)
         fold = (lax.broadcasted_iota(jnp.int32, (NZ * NY * rows, 1), 0) % rows) // (rows // FOLD)
-        for out, weight in ((q_out, qw), (k_out, kw), (v_out, vw)):
+        def project(out, weigh):
             total = None
             for f in range(FOLD):
-                term = jnp.dot(
-                    block_rows,
-                    weight[pl.ds(f * features + c * width, width), :],
-                    preferred_element_type=jnp.float32,
-                )
+                term = weigh(pl.ds(f * features + c * width, width))
                 total = term if f == 0 else jnp.where(fold == f, term, total)
             if c == 0:
                 out[...] = total
             else:
                 out[...] += total
+
+        project(
+            q_out,
+            lambda at: jnp.dot(block_rows, qw[at, :], preferred_element_type=jnp.float32),
+        )
+        project(
+            kv_out,
+            lambda at: lax.dot_general(
+                block_rows, kvw[:, at], (((1,), (1,)), ((), ())), preferred_element_type=jnp.float32
+            ),
+        )
 
     for c in range(CHUNKS):
         forward(c)
@@ -286,7 +300,7 @@
     rows, features = folded.shape
     width = features // CHUNKS
     count = NZ * NY
-    outs = [w.shape[1] for w in (query_weight, key_weight, value_weight)]
+    outs = [query_weight.shape[1], key_weight.shape[1] + value_weight.shape[1]]
     hbm = pl.BlockSpec(memory_space=pl.ANY)
     vmem = pl.BlockSpec(memory_space=pltpu.VMEM)
     dma = pltpu.SemaphoreType.DMA
@@ -294,12 +308,11 @@
         gather_project_kernel,
         out_shape=[jax.ShapeDtypeStruct((count * rows, n), jnp.float32) for n in outs],
         in_specs=[hbm] * 4,
-        out_specs=[vmem] * 3,
+        out_specs=[vmem] * 2,
         scratch_shapes=[
             pltpu.VMEM((CHUNKS, count, rows, width), jnp.bfloat16),
             pltpu.VMEM(query_weight.shape, jnp.bfloat16),
-            pltpu.VMEM(key_weight.shape, jnp.bfloat16),
-            pltpu.VMEM(value_weight.shape, jnp.bfloat16),
+            pltpu.VMEM((outs[1], query_weight.shape[0]), jnp.bfloat16),
             dma((3,)),
             dma((CHUNKS,)),
             dma((CHUNKS, NZ)),
@@ -311,7 +324,7 @@
             collective_id=0, has_side_effects=True, vmem_limit_bytes=48 * 1024 * 1024
         ),
         name="gather_project",
-    )(folded, query_weight, key_weight, value_weight)
+    )(folded, query_weight, key_weight.T, value_weight.T)
 
 
 def project_scatter_kernel(
@@ -359,21 +372,34 @@
             device_id_type=MESH,
         )
 
-    for c in range(CHUNKS):
+    def multiply(c):
         for copy in loads[c]:
             copy.wait()
         product = jnp.dot(heads_ref[...], weight[c], preferred_element_type=jnp.float32)
         terms[c] = product.astype(jnp.bfloat16).reshape(NZ * NY, rows, width)
-        for k in range(NZ - 1, 0, -1):
-            @pl.when(z + k < NZ)
-            def _(c=c, k=k):
-                across(c, z + k).start()
-
-            @pl.when(z >= k)
-            def _(c=c, k=k):
-                across(c, z - k).start()
-
-        across(c, z).start()
+
+    def each_side(group, act):
+        c, k = group // NZ, NZ - 1 - group % NZ
+        if k == 0:
+            act(across(c, z))
+            return
+
+        @pl.when(z + k < NZ)
+        def _():
+            act(across(c, z + k))
+
+        @pl.when(z >= k)
+        def _():
+            act(across(c, z - k))
+
+    def start_side(group):
+        if group < CHUNKS * NZ:
+            if group % NZ == 0:
+                multiply(group // NZ)
+            each_side(group, lambda copy: copy.start())
+
+    for group in range(AHEAD):
+        start_side(group)
 
     def own_pair(c, dest):
         across(c, dest).wait_recv()
@@ -394,7 +420,13 @@
         along(c, dest, step).start()
 
     for c in range(CHUNKS):
-        for k in range(NZ - 1, 0, -1):
+        for k in range(NZ - 1, -1, -1):
+            group = c * NZ + NZ - 1 - k
+            each_side(group, lambda copy: copy.wait_send())
+            start_side(group + AHEAD)
+            if k == 0:
+                break
+
             @pl.when(z + k < NZ)
             def _(c=c, k=k):
                 pass_on(c, z + k, 1, z > 0)
@@ -426,8 +458,6 @@
 
     for c in range(CHUNKS):
         for dest in range(NZ):
-            across(c, dest).wait_send()
-
             @pl.when(dest != z)
             def _(c=c, dest=dest):
                 along(c, dest, 1).wait_send()

time: 108 us -> 99.2 us (0.919)
  local copies, waits for them, and re-layouts: 13.8 us -> 6.8 us
  Pallas kernels: 67.4 us -> 66.2 us
    unnamed x21 -> x15, local copies, waits for them, and re-layouts: 10.8 us -> 3.76 us
    pallas_call x1, Pallas kernels: 30.9 us -> 29.8 us  [gather_project(): pl.pallas_call(gather_project_kernel, out_shape=[jax.ShapeDtypeStruct((co...]
where the time goes in v2:
time: 99.2 us; the launch traced here: 98.9 us
  Pallas kernels  66.2 us (67%)
  waiting for transfers between devices  15.7 us (16%)
  starting transfers between devices  7.62 us (8%)
  local copies, waits for them, and re-layouts  6.8 us (7%)
  matrix products  1.35 us (1%)
  other arithmetic  1.03 us (1%)
    pallas_call x1, Pallas kernels, project_scatter(): pl.pallas_call(project_scatter_kernel, out_shape=jax.ShapeDtypeStruct((ro...  36.5 us
    pallas_call x1, Pallas kernels, gather_project(): pl.pallas_call(gather_project_kernel, out_shape=[jax.ShapeDtypeStruct((co...  29.8 us
    all_to_all x1, waiting for transfers between devices, local_line(): lax.all_to_all(joined.reshape(yz_count * gx_count, rows_here * STEPS, joi...  8.81 us
    all_to_all x1, waiting for transfers between devices, local_line(): lax.all_to_all(sent.reshape(yz_count * gx_count, rows_here * STEPS, HD),...  6.85 us
    all_to_all x1, starting transfers between devices, local_line(): lax.all_to_all(joined.reshape(yz_count * gx_count, rows_here * STEPS, joi...  4.12 us
    unnamed x15, local copies, waits for them, and re-layouts  3.76 us
    all_to_all x1, starting transfers between devices, local_line(): lax.all_to_all(sent.reshape(yz_count * gx_count, rows_here * STEPS, HD),...  3.5 us
  transfers between devices with their start and end apart: 2, of which 2 were waited for; matrix products, arithmetic and copies ran while one was open for 0% of the time, Pallas kernels for 0%

profile of v2, /device:TPU:0, one launch (start us, length us, event | category | flops | bytes accessed | tf_op | source)
XLA Modules:
  0.0 98.9 jit_solution(18354534604565034182)
XLA Ops:
  0.0 0.0 copy-start
  0.0 0.0 copy-start.3
  0.0 0.0 copy-start.2
  0.0 1.2 %copy.10 = bf16[4,3,9216]{2,1,0:T(4,128)(2,1)S(1)} copy(bf16[4,3,9216]{2,0,1:T(4,128)(2,1)} %param.8) | data formatting | bytes 442368 | tf_op args[0]
  1.2 0.2 reshape.148
  1.5 0.1 reshape.149.tokens_ref
  1.5 0.0 copy-done.3
  1.6 0.0 copy-done.2
  1.6 29.8 %gather_project.1 = (f32[384,256]{1,0:T(8,128)S(1)}, f32[384,64]{1,0:T(8,128)S(1)}) custom-call(bf16[48,2304]{1,0:T(8,128)(2,1)S(1)} %reshape.149.tokens_ref, bf16[9216,256]{1,0:T(8,128)(2,1)} %qw_ref.1, bf16[32,9216]{1,0:T(8,128)(2,1)S(1)} %bitcast.47, bf16[32,9216]{1,0:T(8,128)(2,1)S(1)} %bitcast.48), custom_call_target="tpu_custom_call" | custom-call | tf_op jit(solution)/shard_map/gather_project/pallas_call | solution.py:307
  31.4 0.0 copy-start.4
  31.4 0.1 reshape.150
  31.5 0.1 reduce_sum.36
  31.5 0.7 reshape.151
  32.2 4.1 %all-to-all-start = ((f32[16,6,320]{2,1,0:T(8,128)}), f32[16,6,320]{2,1,0:T(8,128)S(1)}, u32[]{:S(2)}, u32[]{:S(2)}) async-start(f32[16,6,320]{2,1,0:T(8,128)} %reshape.151), calls=%async_computation | async-start | bytes 393216 | tf_op jit(solution)/shard_map/all_to_all | solution.py:539
  36.4 0.0 copy-done.4
  36.4 0.1 iota_compare_fusion
  36.5 0.1 add_convert_fusion.2
  36.5 0.0 copy-start.5
  36.5 8.8 %all-to-all-done = f32[16,6,320]{2,1,0:T(8,128)S(1)} async-done(((f32[16,6,320]{2,1,0:T(8,128)}), f32[16,6,320]{2,1,0:T(8,128)S(1)}, u32[]{:S(2)}, u32[]{:S(2)}) %all-to-all-start) | async-done | bytes 122912 | tf_op jit(solution)/shard_map/all_to_all | solution.py:539
  45.4 0.1 slice.43
  45.5 0.1 reshape.161
  45.6 0.1 reshape.162
  45.6 0.1 subtract_convert_fusion.1
  45.8 0.0 copy-done
  45.8 0.6 fusion.23
  46.4 0.2 fusion.24
  46.6 0.2 fusion.11
  46.8 0.2 fusion.15
  47.0 0.0 copy-done.5
  47.0 0.4 fusion.7
  47.4 0.6 broadcast_in_dim.73
  48.1 3.5 %all-to-all-start.1 = ((bf16[16,6,256]{2,1,0:T(8,128)(2,1)}), bf16[16,6,256]{2,1,0:T(8,128)(2,1)S(1)}, u32[]{:S(2)}, u32[]{:S(2)}) async-start(bf16[16,6,256]{2,1,0:T(8,128)(2,1)} %bitcast.16), calls=%async_computation.1 | async-start | bytes 131072 | tf_op jit(solution)/shard_map/all_to_all | solution.py:555
  51.6 6.8 %all-to-all-done.1 = bf16[16,6,256]{2,1,0:T(8,128)(2,1)S(1)} async-done(((bf16[16,6,256]{2,1,0:T(8,128)(2,1)}), bf16[16,6,256]{2,1,0:T(8,128)(2,1)S(1)}, u32[]{:S(2)}, u32[]{:S(2)}) %all-to-all-start.1) | async-done | bytes 49184 | tf_op jit(solution)/shard_map/all_to_all | solution.py:555
  58.5 0.4 broadcast_select_fusion
  58.8 0.2 copy.28
  59.0 0.0 copy-start.1
  59.0 2.3 %copy-done.1 = bf16[256,9216]{1,0:T(8,128)(2,1)S(1)} copy-done((bf16[256,9216]{1,0:T(8,128)(2,1)S(1)}, bf16[256,9216]{1,0:T(8,128)(2,1)}, u32[]{:S(2)}) %copy-start.1) | copy-done | bytes 4718616
  61.3 36.5 %project_scatter.1 = bf16[48,2304]{1,0:T(8,128)(2,1)S(1)} custom-call(bf16[384,1024]{1,0:T(8,128)(2,1)S(1)} %bitcast.46, bf16[256,9216]{1,0:T(8,128)(2,1)S(1)} %copy-done.1), custom_call_target="tpu_custom_call" | custom-call | tf_op jit(solution)/shard_map/project_scatter/pallas_call | solution.py:475
  97.8 0.1 reshape.156
  97.9 0.1 copy.19
  98.0 0.1 reshape.157
  98.1 0.8 copy.20
  (14 shorter events, 0.2 us)
Async XLA Ops:
  0.0 45.8 %copy-start = (bf16[2,1536,256]{2,1,0:T(8,128)(2,1)S(1)}, bf16[2,1536,256]{2,1,0:T(8,128)(2,1)}, u32[]{:S(2)}) copy-start(bf16[2,1536,256]{2,1,0:T(8,128)(2,1)} %param.13) | copy-start | bytes 4718596
  0.0 1.5 %copy-start.3 = (bf16[9216,32]{0,1:T(8,128)(2,1)S(1)}, bf16[9216,32]{0,1:T(8,128)(2,1)}, u32[]{:S(2)}) copy-start(bf16[9216,32]{0,1:T(8,128)(2,1)} %param.11) | copy-start | bytes 1769476
  0.0 1.6 %copy-start.2 = (bf16[9216,32]{0,1:T(8,128)(2,1)S(1)}, bf16[9216,32]{0,1:T(8,128)(2,1)}, u32[]{:S(2)}) copy-start(bf16[9216,32]{0,1:T(8,128)(2,1)} %param.10) | copy-start | bytes 1769476
  31.4 5.0 %copy-start.4 = (s32[2]{0:T(128)S(1)}, s32[2]{0:T(128)}, u32[]{:S(2)}) copy-start(s32[2]{0:T(128)} %param.15) | copy-start | bytes 28
  32.2 13.1 %all-to-all-start = ((f32[16,6,320]{2,1,0:T(8,128)}), f32[16,6,320]{2,1,0:T(8,128)S(1)}, u32[]{:S(2)}, u32[]{:S(2)}) async-start(f32[16,6,320]{2,1,0:T(8,128)} %reshape.151), calls=%async_computation | async-start | bytes 393216 | tf_op jit(solution)/shard_map/all_to_all | solution.py:539
  36.5 10.5 %copy-start.5 = (bf16[2,1536,256]{2,1,0:T(8,128)(2,1)S(1)}, bf16[2,1536,256]{2,1,0:T(8,128)(2,1)}, u32[]{:S(2)}) copy-start(bf16[2,1536,256]{2,1,0:T(8,128)(2,1)} %param.14) | copy-start | bytes 4718596
  48.1 10.4 %all-to-all-start.1 = ((bf16[16,6,256]{2,1,0:T(8,128)(2,1)}), bf16[16,6,256]{2,1,0:T(8,128)(2,1)S(1)}, u32[]{:S(2)}, u32[]{:S(2)}) async-start(bf16[16,6,256]{2,1,0:T(8,128)(2,1)} %bitcast.16), calls=%async_computation.1 | async-start | bytes 131072 | tf_op jit(solution)/shard_map/all_to_all | solution.py:555
  59.0 2.3 %copy-start.1 = (bf16[256,9216]{1,0:T(8,128)(2,1)S(1)}, bf16[256,9216]{1,0:T(8,128)(2,1)}, u32[]{:S(2)}) copy-start(bf16[256,9216]{1,0:T(8,128)(2,1)} %weight_ref.1) | copy-start | bytes 14155780

commit v3 on v2

--- a/solution.py
+++ b/solution.py
@@ -132,7 +132,7 @@
 
 FOLD = 4
 CHUNKS = 3
-AHEAD = 3
+AHEAD = 5
 NZ = 4
 NY = 2
 MESH = pl.DeviceIdType.MESH
@@ -226,27 +226,26 @@
     for copy in loads:
         copy.start()
 
-    def forward(c):
-        for k in range(1, NZ):
-            @pl.when(z >= k)
-            def _(k=k):
-                arrival(c, z - k, y)
-
-                @pl.when(z < NZ - 1)
-                def _():
-                    up(c, z - k).start()
-
-                across(c, z - k).start()
-
-            @pl.when(z + k < NZ)
-            def _(k=k):
-                arrival(c, z + k, y)
-
-                @pl.when(z > 0)
-                def _():
-                    down(c, z + k).start()
-
-                across(c, z + k).start()
+    def forward(c, k):
+        @pl.when(z >= k)
+        def _():
+            arrival(c, z - k, y)
+
+            @pl.when(z < NZ - 1)
+            def _():
+                up(c, z - k).start()
+
+            across(c, z - k).start()
+
+        @pl.when(z + k < NZ)
+        def _():
+            arrival(c, z + k, y)
+
+            @pl.when(z > 0)
+            def _():
+                down(c, z + k).start()
+
+            across(c, z + k).start()
 
     def multiply(c):
         for origin_z in range(NZ):
@@ -274,13 +273,16 @@
             ),
         )
 
-    for c in range(CHUNKS):
-        forward(c)
-        if c == 1:
+    for slot in range(1, CHUNKS + NZ - 1):
+        for c in range(CHUNKS):
+            if 1 <= slot - c < NZ:
+                forward(c, slot - c)
+        done = slot - NZ
+        if done == 0:
             for copy in loads:
                 copy.wait()
-        if c > 0:
-            multiply(c - 1)
+        if done >= 0:
+            multiply(done)
     multiply(CHUNKS - 1)
 
     for c in range(CHUNKS):
@@ -378,8 +380,12 @@
         product = jnp.dot(heads_ref[...], weight[c], preferred_element_type=jnp.float32)
         terms[c] = product.astype(jnp.bfloat16).reshape(NZ * NY, rows, width)
 
+    order = sorted(
+        ((c, k) for c in range(CHUNKS) for k in range(NZ)), key=lambda g: (g[0] - g[1], g[0])
+    )
+
     def each_side(group, act):
-        c, k = group // NZ, NZ - 1 - group % NZ
+        c, k = order[group]
         if k == 0:
             act(across(c, z))
             return
@@ -394,8 +400,8 @@
 
     def start_side(group):
         if group < CHUNKS * NZ:
-            if group % NZ == 0:
-                multiply(group // NZ)
+            if order[group][1] == NZ - 1:
+                multiply(order[group][0])
             each_side(group, lambda copy: copy.start())
 
     for group in range(AHEAD):
@@ -419,14 +425,10 @@
 
         along(c, dest, step).start()
 
-    for c in range(CHUNKS):
-        for k in range(NZ - 1, -1, -1):
-            group = c * NZ + NZ - 1 - k
-            each_side(group, lambda copy: copy.wait_send())
-            start_side(group + AHEAD)
-            if k == 0:
-                break
-
+    for group, (c, k) in enumerate(order):
+        each_side(group, lambda copy: copy.wait_send())
+        start_side(group + AHEAD)
+        if k > 0:
             @pl.when(z + k < NZ)
             def _(c=c, k=k):
                 pass_on(c, z + k, 1, z > 0)
@@ -434,6 +436,8 @@
             @pl.when(z >= k)
             def _(c=c, k=k):
                 pass_on(c, z - k, -1, z < NZ - 1)
+
+            continue
 
         here = pl.ds(c * width, width)
         total = own_pair(c, z)

time: 99.2 us -> 87.8 us (0.89)
  Pallas kernels: 66.2 us -> 55.4 us
    pallas_call x1, Pallas kernels: 36.5 us -> 27 us  [project_scatter(): pl.pallas_call(project_scatter_kernel, out_shape=jax.ShapeDtypeStruct((ro...]
    pallas_call x1, Pallas kernels: 29.8 us -> 28.5 us  [gather_project(): pl.pallas_call(gather_project_kernel, out_shape=[jax.ShapeDtypeStruct((co...]
where the time goes in v3:
time: 87.8 us; the launch traced here: 87.5 us
  Pallas kernels  55.4 us (63%)
  waiting for transfers between devices  15.6 us (18%)
  starting transfers between devices  7.03 us (8%)
  local copies, waits for them, and re-layouts  6.8 us (8%)
  matrix products  1.35 us (2%)
  other arithmetic  1.03 us (1%)
    pallas_call x1, Pallas kernels, gather_project(): pl.pallas_call(gather_project_kernel, out_shape=[jax.ShapeDtypeStruct((co...  28.5 us
    pallas_call x1, Pallas kernels, project_scatter(): pl.pallas_call(project_scatter_kernel, out_shape=jax.ShapeDtypeStruct((ro...  27 us
    all_to_all x1, waiting for transfers between devices, local_line(): lax.all_to_all(joined.reshape(yz_count * gx_count, rows_here * STEPS, joi...  8.78 us
    all_to_all x1, waiting for transfers between devices, local_line(): lax.all_to_all(sent.reshape(yz_count * gx_count, rows_here * STEPS, HD),...  6.85 us
    unnamed x15, local copies, waits for them, and re-layouts  3.76 us
    all_to_all x1, starting transfers between devices, local_line(): lax.all_to_all(joined.reshape(yz_count * gx_count, rows_here * STEPS, joi...  3.52 us
    all_to_all x1, starting transfers between devices, local_line(): lax.all_to_all(sent.reshape(yz_count * gx_count, rows_here * STEPS, HD),...  3.5 us
  transfers between devices with their start and end apart: 2, of which 2 were waited for; matrix products, arithmetic and copies ran while one was open for 0% of the time, Pallas kernels for 0%

profile of v3, /device:TPU:0, one launch (start us, length us, event | category | flops | bytes accessed | tf_op | source)
XLA Modules:
  0.0 87.5 jit_solution(14385499571755376535)
XLA Ops:
  0.0 0.0 copy-start
  0.0 0.0 copy-start.3
  0.0 0.0 copy-start.2
  0.0 1.2 %copy.10 = bf16[4,3,9216]{2,1,0:T(4,128)(2,1)S(1)} copy(bf16[4,3,9216]{2,0,1:T(4,128)(2,1)} %param.8) | data formatting | bytes 442368 | tf_op args[0]
  1.2 0.2 reshape.148
  1.5 0.1 reshape.149.tokens_ref
  1.5 0.0 copy-done.3
  1.6 0.0 copy-done.2
  1.6 28.5 %gather_project.1 = (f32[384,256]{1,0:T(8,128)S(1)}, f32[384,64]{1,0:T(8,128)S(1)}) custom-call(bf16[48,2304]{1,0:T(8,128)(2,1)S(1)} %reshape.149.tokens_ref, bf16[9216,256]{1,0:T(8,128)(2,1)} %qw_ref.1, bf16[32,9216]{1,0:T(8,128)(2,1)S(1)} %bitcast.47, bf16[32,9216]{1,0:T(8,128)(2,1)S(1)} %bitcast.48), custom_call_target="tpu_custom_call" | custom-call | tf_op jit(solution)/shard_map/gather_project/pallas_call | solution.py:309
  30.1 0.0 copy-start.4
  30.1 0.1 reshape.150
  30.2 0.1 reduce_sum.36
  30.3 0.7 reshape.151
  31.0 3.5 %all-to-all-start = ((f32[16,6,320]{2,1,0:T(8,128)}), f32[16,6,320]{2,1,0:T(8,128)S(1)}, u32[]{:S(2)}, u32[]{:S(2)}) async-start(f32[16,6,320]{2,1,0:T(8,128)} %reshape.151), calls=%async_computation | async-start | bytes 393216 | tf_op jit(solution)/shard_map/all_to_all | solution.py:543
  34.5 0.0 copy-done.4
  34.5 0.1 iota_compare_fusion
  34.6 0.1 add_convert_fusion.2
  34.7 0.0 copy-start.5
  34.7 8.8 %all-to-all-done = f32[16,6,320]{2,1,0:T(8,128)S(1)} async-done(((f32[16,6,320]{2,1,0:T(8,128)}), f32[16,6,320]{2,1,0:T(8,128)S(1)}, u32[]{:S(2)}, u32[]{:S(2)}) %all-to-all-start) | async-done | bytes 122912 | tf_op jit(solution)/shard_map/all_to_all | solution.py:543
  43.5 0.1 slice.43
  43.6 0.1 reshape.161
  43.7 0.1 reshape.162
  43.8 0.1 subtract_convert_fusion.1
  43.9 0.0 copy-done
  43.9 0.6 fusion.23
  44.5 0.2 fusion.24
  44.7 0.2 fusion.11
  45.0 0.2 fusion.15
  45.2 0.0 copy-done.5
  45.2 0.4 fusion.7
  45.5 0.6 broadcast_in_dim.73
  46.2 3.5 %all-to-all-start.1 = ((bf16[16,6,256]{2,1,0:T(8,128)(2,1)}), bf16[16,6,256]{2,1,0:T(8,128)(2,1)S(1)}, u32[]{:S(2)}, u32[]{:S(2)}) async-start(bf16[16,6,256]{2,1,0:T(8,128)(2,1)} %bitcast.16), calls=%async_computation.1 | async-start | bytes 131072 | tf_op jit(solution)/shard_map/all_to_all | solution.py:559
  49.7 6.8 %all-to-all-done.1 = bf16[16,6,256]{2,1,0:T(8,128)(2,1)S(1)} async-done(((bf16[16,6,256]{2,1,0:T(8,128)(2,1)}), bf16[16,6,256]{2,1,0:T(8,128)(2,1)S(1)}, u32[]{:S(2)}, u32[]{:S(2)}) %all-to-all-start.1) | async-done | bytes 49184 | tf_op jit(solution)/shard_map/all_to_all | solution.py:559
  56.6 0.4 broadcast_select_fusion
  56.9 0.2 copy.28
  57.1 0.0 copy-start.1
  57.1 2.3 %copy-done.1 = bf16[256,9216]{1,0:T(8,128)(2,1)S(1)} copy-done((bf16[256,9216]{1,0:T(8,128)(2,1)S(1)}, bf16[256,9216]{1,0:T(8,128)(2,1)}, u32[]{:S(2)}) %copy-start.1) | copy-done | bytes 4718616
  59.4 27.0 %project_scatter.1 = bf16[48,2304]{1,0:T(8,128)(2,1)S(1)} custom-call(bf16[384,1024]{1,0:T(8,128)(2,1)S(1)} %bitcast.46, bf16[256,9216]{1,0:T(8,128)(2,1)S(1)} %copy-done.1), custom_call_target="tpu_custom_call" | custom-call | tf_op jit(solution)/shard_map/project_scatter/pallas_call | solution.py:479
  86.4 0.1 reshape.156
  86.5 0.1 copy.19
  86.6 0.1 reshape.157
  86.7 0.8 copy.20
  (14 shorter events, 0.2 us)
Async XLA Ops:
  0.0 43.9 %copy-start = (bf16[2,1536,256]{2,1,0:T(8,128)(2,1)S(1)}, bf16[2,1536,256]{2,1,0:T(8,128)(2,1)}, u32[]{:S(2)}) copy-start(bf16[2,1536,256]{2,1,0:T(8,128)(2,1)} %param.13) | copy-start | bytes 4718596
  0.0 1.5 %copy-start.3 = (bf16[9216,32]{0,1:T(8,128)(2,1)S(1)}, bf16[9216,32]{0,1:T(8,128)(2,1)}, u32[]{:S(2)}) copy-start(bf16[9216,32]{0,1:T(8,128)(2,1)} %param.11) | copy-start | bytes 1769476
  0.0 1.6 %copy-start.2 = (bf16[9216,32]{0,1:T(8,128)(2,1)S(1)}, bf16[9216,32]{0,1:T(8,128)(2,1)}, u32[]{:S(2)}) copy-start(bf16[9216,32]{0,1:T(8,128)(2,1)} %param.10) | copy-start | bytes 1769476
  30.1 4.4 %copy-start.4 = (s32[2]{0:T(128)S(1)}, s32[2]{0:T(128)}, u32[]{:S(2)}) copy-start(s32[2]{0:T(128)} %param.15) | copy-start | bytes 28
  31.0 12.5 %all-to-all-start = ((f32[16,6,320]{2,1,0:T(8,128)}), f32[16,6,320]{2,1,0:T(8,128)S(1)}, u32[]{:S(2)}, u32[]{:S(2)}) async-start(f32[16,6,320]{2,1,0:T(8,128)} %reshape.151), calls=%async_computation | async-start | bytes 393216 | tf_op jit(solution)/shard_map/all_to_all | solution.py:543
  34.7 10.5 %copy-start.5 = (bf16[2,1536,256]{2,1,0:T(8,128)(2,1)S(1)}, bf16[2,1536,256]{2,1,0:T(8,128)(2,1)}, u32[]{:S(2)}) copy-start(bf16[2,1536,256]{2,1,0:T(8,128)(2,1)} %param.14) | copy-start | bytes 4718596
  46.2 10.4 %all-to-all-start.1 = ((bf16[16,6,256]{2,1,0:T(8,128)(2,1)}), bf16[16,6,256]{2,1,0:T(8,128)(2,1)S(1)}, u32[]{:S(2)}, u32[]{:S(2)}) async-start(bf16[16,6,256]{2,1,0:T(8,128)(2,1)} %bitcast.16), calls=%async_computation.1 | async-start | bytes 131072 | tf_op jit(solution)/shard_map/all_to_all | solution.py:559
  57.1 2.3 %copy-start.1 = (bf16[256,9216]{1,0:T(8,128)(2,1)S(1)}, bf16[256,9216]{1,0:T(8,128)(2,1)}, u32[]{:S(2)}) copy-start(bf16[256,9216]{1,0:T(8,128)(2,1)} %weight_ref.1) | copy-start | bytes 14155780

commit v4 on v3

--- a/solution.py
+++ b/solution.py
@@ -131,8 +131,8 @@
 
 
 FOLD = 4
-CHUNKS = 3
-AHEAD = 5
+CHUNKS = 6
+AHEAD = 8
 NZ = 4
 NY = 2
 MESH = pl.DeviceIdType.MESH
@@ -323,7 +323,7 @@
             dma((CHUNKS, count)),
         ],
         compiler_params=pltpu.CompilerParams(
-            collective_id=0, has_side_effects=True, vmem_limit_bytes=48 * 1024 * 1024
+            collective_id=0, has_side_effects=True, vmem_limit_bytes=60 * 1024 * 1024
         ),
         name="gather_project",
     )(folded, query_weight, key_weight.T, value_weight.T)
@@ -495,7 +495,7 @@
             sems,
         ],
         compiler_params=pltpu.CompilerParams(
-            collective_id=1, has_side_effects=True, vmem_limit_bytes=48 * 1024 * 1024
+            collective_id=1, has_side_effects=True, vmem_limit_bytes=60 * 1024 * 1024
         ),
         name="project_scatter",
     )(heads, out_weight)

time: 87.8 us -> 104 us (1.18)
  Pallas kernels: 55.4 us -> 69.6 us
  other arithmetic: 1.03 us -> 2.13 us
    pallas_call x1, Pallas kernels: 27 us -> 34.8 us  [project_scatter(): pl.pallas_call(project_scatter_kernel, out_shape=jax.ShapeDtypeStruct((ro...]
    pallas_call x1, Pallas kernels: 28.5 us -> 34.8 us  [gather_project(): pl.pallas_call(gather_project_kernel, out_shape=[jax.ShapeDtypeStruct((co...]
    unnamed x15 -> x9, local copies, waits for them, and re-layouts: 3.76 us -> 2.28 us
    concatenate x1, other arithmetic: 0.04 us -> 1.14 us  [local_line(): joined = jnp.concatenate(parts, axis=1)]
where the time goes in v4:
time: 104 us; the launch traced here: 103 us
  Pallas kernels  69.6 us (67%)
  waiting for transfers between devices  15.7 us (15%)
  starting transfers between devices  7.4 us (7%)
  local copies, waits for them, and re-layouts  6.94 us (7%)
  other arithmetic  2.13 us (2%)
  matrix products  1.35 us (1%)
    pallas_call x1, Pallas kernels, gather_project(): pl.pallas_call(gather_project_kernel, out_shape=[jax.ShapeDtypeStruct((co...  34.8 us
    pallas_call x1, Pallas kernels, project_scatter(): pl.pallas_call(project_scatter_kernel, out_shape=jax.ShapeDtypeStruct((ro...  34.8 us
    all_to_all x1, waiting for transfers between devices, local_line(): lax.all_to_all(joined.reshape(yz_count * gx_count, rows_here * STEPS, joi...  8.81 us
    all_to_all x1, waiting for transfers between devices, local_line(): lax.all_to_all(sent.reshape(yz_count * gx_count, rows_here * STEPS, HD),...  6.85 us
    all_to_all x1, starting transfers between devices, local_line(): lax.all_to_all(joined.reshape(yz_count * gx_count, rows_here * STEPS, joi...  3.89 us
    all_to_all x1, starting transfers between devices, local_line(): lax.all_to_all(sent.reshape(yz_count * gx_count, rows_here * STEPS, HD),...  3.5 us
    unnamed x9, local copies, waits for them, and re-layouts  2.28 us
  transfers between devices with their start and end apart: 2, of which 2 were waited for; matrix products, arithmetic and copies ran while one was open for 0% of the time, Pallas kernels for 0%

profile of v4, /device:TPU:0, one launch (start us, length us, event | category | flops | bytes accessed | tf_op | source)
XLA Modules:
  0.0 103.2 jit_solution(8073275006117985511)
XLA Ops:
  0.0 0.0 copy-start
  0.0 1.2 %copy.10 = bf16[4,3,9216]{2,1,0:T(4,128)(2,1)S(1)} copy(bf16[4,3,9216]{2,0,1:T(4,128)(2,1)} %param.8) | data formatting | bytes 442368 | tf_op args[0]
  1.2 0.2 reshape.148
  1.4 0.7 reshape.149.tokens_ref
  2.2 34.8 %gather_project.1 = (f32[384,256]{1,0:T(8,128)}, f32[384,64]{1,0:T(8,128)}) custom-call(bf16[48,2304]{1,0:T(8,128)(2,1)} %reshape.149.tokens_ref, bf16[9216,256]{1,0:T(8,128)(2,1)} %qw_ref.1, bf16[32,9216]{1,0:T(8,128)(2,1)} %bitcast.50, bf16[32,9216]{1,0:T(8,128)(2,1)} %bitcast.51), custom_call_target="tpu_custom_call" | custom-call | tf_op jit(solution)/shard_map/gather_project/pallas_call | solution.py:309
  37.0 1.1 %pad_maximum_fusion = f32[384,320]{1,0:T(8,128)S(1)} fusion(f32[384,64]{1,0:T(8,128)} %get-tuple-element.8, f32[384,256]{1,0:T(8,128)} %get-tuple-element.7), kind=kLoop, calls=%fused_computation.10 | loop fusion | flops 122880 | bytes 983040 | tf_op jit(solution)/shard_map/concatenate | solution.py:541
  38.2 0.0 copy-start.1
  38.2 0.1 reshape.150
  38.2 0.1 reduce_sum.36
  38.3 0.7 reshape.151
  39.0 3.9 %all-to-all-start = ((f32[16,6,320]{2,1,0:T(8,128)}), f32[16,6,320]{2,1,0:T(8,128)S(1)}, u32[]{:S(2)}, u32[]{:S(2)}) async-start(f32[16,6,320]{2,1,0:T(8,128)} %reshape.151), calls=%async_computation | async-start | bytes 393216 | tf_op jit(solution)/shard_map/all_to_all | solution.py:543
  42.9 0.0 copy-done.1
  42.9 0.1 iota_compare_fusion
  43.0 0.1 add_convert_fusion.2
  43.1 0.0 copy-start.2
  43.1 8.8 %all-to-all-done = f32[16,6,320]{2,1,0:T(8,128)S(1)} async-done(((f32[16,6,320]{2,1,0:T(8,128)}), f32[16,6,320]{2,1,0:T(8,128)S(1)}, u32[]{:S(2)}, u32[]{:S(2)}) %all-to-all-start) | async-done | bytes 122912 | tf_op jit(solution)/shard_map/all_to_all | solution.py:543
  51.9 0.1 slice.43
  52.0 0.1 reshape.161
  52.1 0.1 reshape.162
  52.2 0.1 subtract_convert_fusion.1
  52.3 0.0 copy-done
  52.4 0.6 fusion.23
  53.0 0.2 fusion.24
  53.2 0.2 fusion.11
  53.4 0.2 fusion.15
  53.6 0.0 copy-done.2
  53.6 0.4 fusion.7
  54.0 0.6 broadcast_in_dim.73
  54.6 3.5 %all-to-all-start.1 = ((bf16[16,6,256]{2,1,0:T(8,128)(2,1)}), bf16[16,6,256]{2,1,0:T(8,128)(2,1)S(1)}, u32[]{:S(2)}, u32[]{:S(2)}) async-start(bf16[16,6,256]{2,1,0:T(8,128)(2,1)} %bitcast.16), calls=%async_computation.1 | async-start | bytes 131072 | tf_op jit(solution)/shard_map/all_to_all | solution.py:559
  58.1 6.8 %all-to-all-done.1 = bf16[16,6,256]{2,1,0:T(8,128)(2,1)S(1)} async-done(((bf16[16,6,256]{2,1,0:T(8,128)(2,1)}), bf16[16,6,256]{2,1,0:T(8,128)(2,1)S(1)}, u32[]{:S(2)}, u32[]{:S(2)}) %all-to-all-start.1) | async-done | bytes 49184 | tf_op jit(solution)/shard_map/all_to_all | solution.py:559
  65.0 0.4 broadcast_select_fusion
  65.4 1.0 %copy.28 = bf16[48,8,4,256]{3,1,2,0:T(8,128)(2,1)} copy(bf16[48,8,4,256]{3,2,1,0:T(4,128)(2,1)S(1)} %bitcast.46) | data formatting | bytes 1572864
  66.4 34.8 %project_scatter.1 = bf16[48,2304]{1,0:T(8,128)(2,1)} custom-call(bf16[384,1024]{1,0:T(8,128)(2,1)} %bitcast.47, bf16[256,9216]{1,0:T(8,128)(2,1)} %weight_ref.1), custom_call_target="tpu_custom_call" | custom-call | tf_op jit(solution)/shard_map/project_scatter/pallas_call | solution.py:479
  101.2 1.0 reshape.156
  102.2 0.1 copy.19
  102.3 0.1 reshape.157
  102.4 0.8 copy.20
  (13 shorter events, 0.2 us)
Async XLA Ops:
  0.0 52.3 %copy-start = (bf16[2,1536,256]{2,1,0:T(8,128)(2,1)S(1)}, bf16[2,1536,256]{2,1,0:T(8,128)(2,1)}, u32[]{:S(2)}) copy-start(bf16[2,1536,256]{2,1,0:T(8,128)(2,1)} %param.13) | copy-start | bytes 4718596
  38.2 4.8 %copy-start.1 = (s32[2]{0:T(128)S(1)}, s32[2]{0:T(128)}, u32[]{:S(2)}) copy-start(s32[2]{0:T(128)} %param.15) | copy-start | bytes 28
  39.0 12.9 %all-to-all-start = ((f32[16,6,320]{2,1,0:T(8,128)}), f32[16,6,320]{2,1,0:T(8,128)S(1)}, u32[]{:S(2)}, u32[]{:S(2)}) async-start(f32[16,6,320]{2,1,0:T(8,128)} %reshape.151), calls=%async_computation | async-start | bytes 393216 | tf_op jit(solution)/shard_map/all_to_all | solution.py:543
  43.1 10.5 %copy-start.2 = (bf16[2,1536,256]{2,1,0:T(8,128)(2,1)S(1)}, bf16[2,1536,256]{2,1,0:T(8,128)(2,1)}, u32[]{:S(2)}) copy-start(bf16[2,1536,256]{2,1,0:T(8,128)(2,1)} %param.14) | copy-start | bytes 4718596
  54.6 10.4 %all-to-all-start.1 = ((bf16[16,6,256]{2,1,0:T(8,128)(2,1)}), bf16[16,6,256]{2,1,0:T(8,128)(2,1)S(1)}, u32[]{:S(2)}, u32[]{:S(2)}) async-start(bf16[16,6,256]{2,1,0:T(8,128)(2,1)} %bitcast.16), calls=%async_computation.1 | async-start | bytes 131072 | tf_op jit(solution)/shard_map/all_to_all | solution.py:559
